TPU v7x, 32 devices: a whole 2x2x4 slice. The times are simulated.
32 devices in a mesh: gx: 8 (over y, x, core), gy: 4 (over z).
Axes of the slice: x: 2, y: 2, z: 4, core: 2. Of those that a mesh axis runs over, the one named last changes fastest.
Arguments:
- estimate: float32 [2, 1024, 512], P(None, 'gx', 'gy'), may hold values from 0.24 to 5.3
- views: bfloat16 [4, 2, 1024, 512], P(None, None, 'gx', 'gy'), may hold values from 0.18 to 7
- psf_rows: float32 [4, 31], replicated, may hold values from 0.05 to 1
- psf_cols: float32 [4, 31], replicated, may hold values from 0.05 to 1
- shifts: int32 [4, 128], P(None, 'gx'), may hold values from 0 to 3, as said below
- codes: int32 [4, 128, 4], P(None, 'gx', 'gy'), may hold values from 0 to 15
Outputs:
- updated: float32 [2, 1024, 512], P(None, 'gx', 'gy')
Inputs may be any that keep to these rules, and one draw needn't show every extreme that they name: `shifts`: within each view and each group of 16 consecutive block rows that starts at a multiple of 16, no displacement occurs more than 5 times, and one occurs exactly 5 times.
All inputs are finite; a program needn't handle non-finite values.
Results may differ from a plain program's by a relative error of at most 0.0003.
Values sent between devices are 32-bit elements; how exact they have to be, the bound alone decides.
A program may use at most 64 MiB of HBM per device.

v0:
```python
import functools

import jax
import jax.numpy as jnp
from jax import lax
from jax.experimental import pallas as pl
from jax.experimental.pallas import tpu as pltpu
from jax.sharding import PartitionSpec as P

ITERS = 2
MESH = pl.DeviceIdType.MESH
F32 = jnp.float32
BF16 = jnp.bfloat16
HALO = 4
NEAR = 2


def with_halo(block, sides, width):
    for axis, dim in sides:
        count = lax.axis_size(axis)
        forward = [(i, i + 1) for i in range(count - 1)]
        backward = [(target, source) for source, target in forward]
        low = lax.ppermute(
            lax.slice_in_dim(block, block.shape[dim] - width, None, axis=dim), axis, forward
        )
        high = lax.ppermute(lax.slice_in_dim(block, 0, width, axis=dim), axis, backward)
        block = jnp.concatenate([low, block, high], axis=dim)
    return block


def shift_in(values, fraction):
    last = values.shape[-1] - 1
    column = lax.broadcasted_iota(jnp.int32, values.shape, values.ndim - 1)
    following = jnp.concatenate([values[..., 1:], values[..., -1:]], axis=-1)
    return jnp.where(column < last, (1.0 - fraction) * values + fraction * following, values)


def shift_back(values, fraction):
    last = values.shape[-1] - 1
    column = lax.broadcasted_iota(jnp.int32, values.shape, values.ndim - 1)
    preceding = jnp.concatenate([jnp.zeros_like(values[..., :1]), values[..., :-1]], axis=-1)
    own_part = jnp.where(column < last, (1.0 - fraction) * values, values)
    return own_part + fraction * preceding


def smooth_rows(padded, taps, count):
    total = taps[0] * padded[..., 0:count, :]
    for offset in range(1, taps.shape[0]):
        total = total + taps[offset] * padded[..., offset : offset + count, :]
    return total


def smooth_cols(padded, taps, count):
    total = taps[0] * padded[..., 0:count]
    for offset in range(1, taps.shape[0]):
        total = total + taps[offset] * padded[..., offset : offset + count]
    return total


def tile_body(estimate, views, psf_rows, psf_cols, shifts, codes):
    highest = lax.Precision.HIGHEST
    groups = lax.axis_size("gy")
    column = lax.axis_index("gy")
    views_n, depth, tile_rows, tile_cols = views.shape
    blocks_n = shifts.shape[1]
    block_rows = tile_rows // blocks_n
    capacity = 1 + (blocks_n + groups - 2) // groups
    tap_count = psf_rows.shape[1]
    half = tap_count // 2
    kern_rows = psf_rows / jnp.sum(psf_rows, axis=1, keepdims=True)
    kern_cols = psf_cols / jnp.sum(psf_cols, axis=1, keepdims=True)
    taps_rows = kern_rows.T.reshape(tap_count, views_n, 1, 1, 1)
    taps_cols = kern_cols.T.reshape(tap_count, views_n, 1, 1, 1)
    flipped_rows = kern_rows[:, ::-1].T.reshape(tap_count, views_n, 1, 1, 1)
    flipped_cols = kern_cols[:, ::-1].T.reshape(tap_count, views_n, 1, 1, 1)
    fraction = (codes[:, :, 0].astype(jnp.float32) / 16.0)[:, None, :, None, None]
    block_ids = jnp.arange(blocks_n, dtype=jnp.int32)
    same_shift = shifts[:, :, None] == shifts[:, None, :]
    earlier = block_ids[None, None, :] < block_ids[None, :, None]
    slot_rank = jnp.sum((same_shift & earlier).astype(jnp.int32), axis=2)
    peer_ids = jnp.arange(groups, dtype=jnp.int32)
    slot_ids = jnp.arange(capacity, dtype=jnp.int32)
    source_peer = (column + shifts) % groups
    target_peer = (column - shifts) % groups
    send_hot = (
        (peer_ids[None, :, None, None] == target_peer[:, None, None, :])
        & (slot_ids[None, None, :, None] == slot_rank[:, None, None, :])
    ).astype(jnp.float32)
    recv_hot = (
        (peer_ids[None, None, :, None] == source_peer[:, :, None, None])
        & (slot_ids[None, None, None, :] == slot_rank[:, :, None, None])
    ).astype(jnp.float32)
    for sweep in range(ITERS):
        blocked = estimate.reshape(depth, blocks_n, block_rows, tile_cols)
        outgoing = jnp.einsum("vpqk,zkrw->pvqzrw", send_hot, blocked, precision=highest)
        arriving = lax.all_to_all(outgoing, "gy", split_axis=0, concat_axis=0, tiled=True)
        view_blocks = jnp.einsum("vkpq,pvqzrw->vzkrw", recv_hot, arriving, precision=highest)
        view_est = shift_in(view_blocks, fraction).reshape(views_n, depth, tile_rows, tile_cols)
        padded = with_halo(view_est, (("gx", 2), ("gy", 3)), half)
        rows_done = smooth_rows(padded, taps_rows, tile_rows)
        blurred = smooth_cols(rows_done, taps_cols, tile_cols)
        ratio = views.astype(jnp.float32) / blurred
        padded_ratio = with_halo(ratio, (("gx", 2), ("gy", 3)), half)
        rows_back = smooth_rows(padded_ratio, flipped_rows, tile_rows)
        back = smooth_cols(rows_back, flipped_cols, tile_cols)
        returned = shift_back(
            back.reshape(views_n, depth, blocks_n, block_rows, tile_cols), fraction
        )
        leaving = jnp.einsum("vkpq,vzkrw->pvqzrw", recv_hot, returned, precision=highest)
        coming = lax.all_to_all(leaving, "gy", split_axis=0, concat_axis=0, tiled=True)
        summed = jnp.einsum("vpqk,pvqzrw->zkrw", send_hot, coming, precision=highest)
        estimate = estimate * (summed.reshape(depth, tile_rows, tile_cols) / views_n)
    return estimate


def split_store(ref, index, value):
    high = value.astype(BF16)
    ref[(0,) + index] = high
    ref[(1,) + index] = (value - high.astype(F32)).astype(BF16)


def product(left, right, dims):
    return lax.dot_general(left, right, (dims, ((), ())), preferred_element_type=F32)


def split(value):
    high = value.astype(BF16)
    return high, (value - high.astype(F32)).astype(BF16)


def rows_by(band, field):
    high, low = split(field)
    dims = ((1,), (0,))
    return (
        product(band[0], high, dims) + product(band[0], low, dims) + product(band[1], high, dims)
    )


def cols_by(field, band, side):
    width = band.shape[-1] // 2
    rows = field.shape[0]
    count = field.shape[1] // width - 1
    high, low = split(field)
    windows = [part[:, j * width : (j + 2) * width] for part in (high, low) for j in range(count)]
    dims = ((1,), (side,))
    first = product(jnp.concatenate(windows, axis=0), band[0], dims)
    second = product(jnp.concatenate(windows[:count], axis=0), band[1], dims)
    done = first[: count * rows] + first[count * rows :] + second
    done = [done[j * rows : (j + 1) * rows] for j in range(count)]
    lane = lax.broadcasted_iota(jnp.int32, (rows, width), 1)
    tiles = [done[0][:, :width]]
    for j in range(count - 1):
        tiles.append(jnp.where(lane < width // 2, done[j][:, width:], done[j + 1][:, :width]))
    tiles.append(done[-1][:, width:])
    return tiles


def taps_of(ref, view):
    taps = [ref[view, t] for t in range(ref.shape[1])]
    return taps, functools.reduce(lambda a, b: a + b, taps)


def banded(taps, total, offset):
    value = jnp.zeros(offset.shape, F32)
    for t, tap in enumerate(taps):
        value = jnp.where(offset == t, tap, value)
    return value / jnp.full(offset.shape, total, F32)


def kernel(
    gx_n, gy_n, est_ref, views_ref, meta_ref, psf_rows_ref, psf_cols_ref, out_ref,
    est_band, views_out, views_band, meta_band, lines, frac_full, shift_full, out_own, out_in,
    band_fwd, band_back, band_cols,
    gather_s, gather_r, halo_s, halo_r, views_s, views_r, near_s, near_r,
    meta_s, meta_r, edge_s, edge_r, out_s, out_r,
):
    views_n, depth, _, width = views_ref.shape
    blocks_n, block_rows = est_ref.shape[1:3]
    part_n = blocks_n // 2
    part_rows = part_n * block_rows
    band_rows = (part_n + 2 * HALO) * block_rows
    near_rows = (part_n + 2 * NEAR) * block_rows
    half = psf_rows_ref.shape[1] // 2
    g = lax.axis_index("gx")
    c = lax.axis_index("gy")

    def place_of(device):
        return device // 2, lax.rem(device + g, 2)

    plane, h = place_of(c)
    peers = [lax.rem(c + k, gy_n) for k in range(1, gy_n)]
    partner = {"gy": c + 1 - 2 * lax.rem(c, 2)}
    beside = {"gx": lax.rem(g - 1 + 2 * h + gx_n, gx_n)}
    pending = []

    def send(src, dst, send_sem, recv_sem, target):
        copy = pltpu.make_async_remote_copy(
            src_ref=src, dst_ref=dst, send_sem=send_sem, recv_sem=recv_sem,
            device_id=target, device_id_type=MESH,
        )
        copy.start()
        pending.append(copy)
        return copy

    barrier = pltpu.get_barrier_semaphore()
    for target in [{"gy": p} for p in peers] + [beside]:
        pl.semaphore_signal(barrier, inc=1, device_id=target, device_id_type=MESH)
    for view in range(views_n):
        for layer in range(depth):
            views_out[view, layer] = (
                views_ref[view, layer].astype(F32).reshape(blocks_n, block_rows, width)
            )
    pl.semaphore_wait(barrier, gy_n)

    meta_copies = [
        send(meta_ref, meta_band.at[c, pl.ds(1, 2)], meta_s.at[k], meta_r.at[k], {"gy": p})
        for k, p in enumerate(peers)
    ]
    est_n = part_n + HALO
    view_n = part_n + NEAR
    gathers = []
    for k, p in enumerate(peers):
        layer, other = place_of(p)
        gathers.append(
            send(
                est_ref.at[layer, pl.ds(HALO * other, est_n)],
                est_band.at[0, c, pl.ds(HALO - HALO * other, est_n)],
                gather_s.at[k], gather_r.at[k], {"gy": p},
            )
        )
    view_copies = []
    for view in range(views_n):
        copies = []
        for k, p in enumerate(peers):
            layer, other = place_of(p)
            copies.append(
                send(
                    views_out.at[view, layer, pl.ds((part_n - NEAR) * other, view_n)],
                    views_band.at[view, c, pl.ds(NEAR - NEAR * other, view_n)],
                    views_s.at[view, k], views_r.at[view, k], {"gy": p},
                )
            )
        view_copies.append(copies)
    meta_band[c, pl.ds(1, 2)] = meta_ref[...]
    est_band[0, c, pl.ds(HALO - HALO * h, est_n)] = est_ref[plane, pl.ds(HALO * h, est_n)]
    for view in range(views_n):
        views_band[view, c, pl.ds(NEAR - NEAR * h, view_n)] = views_out[
            view, plane, pl.ds((part_n - NEAR) * h, view_n)
        ]

    for copy in meta_copies:
        copy.wait_recv()
    edge = send(
        meta_band.at[:, 1 + h], meta_band.at[:, 3 - 3 * h], edge_s.at[0], edge_r.at[0], beside
    )
    for copy in gathers:
        copy.wait_recv()
    halo = send(
        est_band.at[0, :, pl.ds(HALO + (part_n - HALO) * h, HALO)],
        est_band.at[0, :, pl.ds((part_n + HALO) * (1 - h), HALO)],
        halo_s.at[0], halo_r.at[0], beside,
    )

    first_row = jnp.where((g == 0) & (h == 0), 0, -HALO * block_rows)
    last_row = jnp.where((g == gx_n - 1) & (h == 1), part_rows, part_rows + HALO * block_rows)
    for view in range(views_n):
        taps, total = taps_of(psf_rows_ref, view)
        row = lax.broadcasted_iota(jnp.int32, (near_rows, band_rows), 0) - NEAR * block_rows
        col = lax.broadcasted_iota(jnp.int32, (near_rows, band_rows), 1) - HALO * block_rows
        inside = (col >= first_row) & (col < last_row)
        outer = (row < first_row) | (row >= last_row)
        value = banded(taps, total, col - row + half)
        split_store(band_fwd.at[view], (), jnp.where(inside | outer, value, 0.0))
        row = lax.broadcasted_iota(jnp.int32, (part_rows, near_rows), 0)
        col = lax.broadcasted_iota(jnp.int32, (part_rows, near_rows), 1) - NEAR * block_rows
        inside = (col >= first_row) & (col < last_row)
        value = banded(taps, total, row - col + half)
        split_store(band_back.at[view], (), jnp.where(inside, value, 0.0))
        taps, total = taps_of(psf_cols_ref, view)
        row = lax.broadcasted_iota(jnp.int32, (width, width), 0)
        col = lax.broadcasted_iota(jnp.int32, (width, width), 1)
        value = banded(taps, total, row - col + half)
        low, high = pl.ds(0, width), pl.ds(width, width)
        split_store(band_cols.at[view], (low, low), value)
        split_store(band_cols.at[view], (high, high), value)
        row, col = row[:16], col[:16]
        blank = jnp.zeros((width - 16, width), F32)
        value = banded(taps, total, row + width - col + half)
        split_store(band_cols.at[view], (high, low), jnp.concatenate([value, blank], axis=0))
        value = banded(taps, total, row - 16 - col + half)
        split_store(band_cols.at[view], (low, high), jnp.concatenate([blank, value], axis=0))

    edge.wait_recv()
    for j in range(gy_n):
        found = meta_band[j].reshape(4 * 8, width)
        for view in range(views_n):
            lines[view, j] = jnp.broadcast_to(found[:, view : view + 1], found.shape)
            if j == 0:
                near = found[:, views_n + view : views_n + view + 1]
                lines[view, gy_n] = jnp.broadcast_to(near, found.shape)

    def spread(b, carry):
        place = pl.ds(b + 8 - HALO + part_n * h, 1)
        for view in range(views_n):
            for j in range(gy_n):
                frac_full[view, j, b] = jnp.broadcast_to(
                    lines[view, j, place, :], (block_rows, width)
                )
            shift_full[view, b] = jnp.broadcast_to(
                lines[view, gy_n, place, :], (block_rows, width)
            )
        return carry

    lax.fori_loop(0, part_n + 2 * HALO, spread, 0)
    halo.wait_recv()

    def pick(shift, tiles, first, sign):
        value = tiles[first % gy_n]
        for k in range(1, gy_n):
            value = jnp.where(shift == float(k), tiles[(first + sign * k) % gy_n], value)
        return value

    own = pl.ds(HALO, part_n)
    for sweep in range(ITERS):
        sums = None
        for view in range(views_n):
            if sweep == 0:
                for copy in view_copies[view]:
                    copy.wait_recv()
                near = send(
                    views_band.at[view, :, pl.ds(NEAR + (part_n - NEAR) * h, NEAR)],
                    views_band.at[view, :, pl.ds((part_n + NEAR) * (1 - h), NEAR)],
                    near_s.at[view], near_r.at[view], beside,
                )
            shift = shift_full[view]
            lane = lax.broadcasted_iota(jnp.int32, (band_rows, width), 1)
            tiles = [est_band[sweep, j] for j in range(gy_n)]
            parts = []
            for j in range(gy_n):
                moved = pick(shift, tiles, j, 1).reshape(band_rows, width)
                fraction = frac_full[view, j].reshape(band_rows, width)
                fraction = jnp.where(lane < width - 1, fraction, 0.0)
                following = pltpu.roll(moved, width - 1, 1)
                parts.append((1.0 - fraction) * moved + fraction * following)
            rows_done = rows_by(band_fwd.at[view], jnp.concatenate(parts, axis=1))
            blurred = cols_by(rows_done, band_cols.at[view], 0)
            if sweep == 0:
                near.wait_recv()
            ratio = [
                views_band[view, j].reshape(near_rows, width) / blurred[j] for j in range(gy_n)
            ]
            rows_back = rows_by(band_back.at[view], jnp.concatenate(ratio, axis=1))
            back = cols_by(rows_back, band_cols.at[view], 1)
            lane = lax.broadcasted_iota(jnp.int32, (part_rows, width), 1)
            returned = []
            for j in range(gy_n):
                fraction = frac_full[view, j, own].reshape(part_rows, width)
                kept = jnp.where(lane < width - 1, 1.0 - fraction, 1.0)
                passed = jnp.where(lane > 0, fraction, 0.0)
                value = kept * back[j] + passed * pltpu.roll(back[j], 1, 1)
                returned.append(value.reshape(part_n, block_rows, width))
            shift = shift_full[view, own]
            homes = [pick(shift, returned, j, -1) for j in range(gy_n)]
            sums = homes if sums is None else [a + b for a, b in zip(sums, homes)]
        updated = [est_band[sweep, j, own] * (sums[j] / views_n) for j in range(gy_n)]
        if sweep + 1 < ITERS:
            for j in range(gy_n):
                est_band[sweep + 1, j, own] = updated[j]
            band = est_band.at[sweep + 1]
            halos = [
                send(
                    band.at[:, pl.ds(part_n - (part_n - HALO) * h, HALO)],
                    band.at[:, pl.ds((part_n + HALO) * h, HALO)],
                    halo_s.at[2 * sweep + 1], halo_r.at[2 * sweep + 1], partner,
                ),
                send(
                    band.at[:, pl.ds(HALO + (part_n - HALO) * h, HALO)],
                    band.at[:, pl.ds((part_n + HALO) * (1 - h), HALO)],
                    halo_s.at[2 * sweep + 2], halo_r.at[2 * sweep + 2], beside,
                ),
            ]
            for copy in halos:
                copy.wait_recv()
    for j in range(gy_n):
        out_own[j] = updated[j]
    place = pl.ds(part_n * h, part_n)
    outs = [
        send(out_own.at[p], out_in.at[plane, place], out_s.at[k], out_r.at[k], {"gy": p})
        for k, p in enumerate(peers)
    ]
    out_in[plane, place] = out_own[c]
    for copy in outs:
        copy.wait_recv()
    out_ref[...] = out_in[...]
    for copy in pending:
        copy.wait_send()


def band_body(gx_n, gy_n, estimate, views, psf_rows, psf_cols, shifts, codes):
    views_n, depth, tile_rows, width = views.shape
    blocks_n = shifts.shape[1]
    block_rows = tile_rows // blocks_n
    fraction = codes[:, :, 0].astype(F32) / 16.0
    meta = jnp.concatenate([fraction, shifts.astype(F32)], axis=0).T
    meta = jnp.pad(meta, ((0, 0), (0, width - 2 * views_n))).reshape(2, 8, width)
    part_n = blocks_n // 2
    part_rows = part_n * block_rows
    near_rows = part_rows + 2 * NEAR * block_rows
    band_rows = part_rows + 2 * HALO * block_rows
    others = gy_n - 1
    vmem = pltpu.VMEM
    dma = pltpu.SemaphoreType.DMA
    out = pl.pallas_call(
        functools.partial(kernel, gx_n, gy_n),
        out_shape=jax.ShapeDtypeStruct((depth, blocks_n, block_rows, width), F32),
        in_specs=[pl.BlockSpec(memory_space=pltpu.VMEM)] * 3
        + [pl.BlockSpec(memory_space=pltpu.SMEM)] * 2,
        out_specs=pl.BlockSpec(memory_space=pltpu.VMEM),
        scratch_shapes=[
            vmem((ITERS, gy_n, part_n + 2 * HALO, block_rows, width), F32),
            vmem((views_n, depth, blocks_n, block_rows, width), F32),
            vmem((views_n, gy_n, part_n + 2 * NEAR, block_rows, width), F32),
            vmem((gy_n, 4, 8, width), F32),
            vmem((views_n, gy_n + 1, 4 * 8, width), F32),
            vmem((views_n, gy_n, part_n + 2 * HALO, block_rows, width), F32),
            vmem((views_n, part_n + 2 * HALO, block_rows, width), F32),
            vmem((gy_n, part_n, block_rows, width), F32),
            vmem((depth, blocks_n, block_rows, width), F32),
            vmem((views_n, 2, near_rows, band_rows), BF16),
            vmem((views_n, 2, part_rows, near_rows), BF16),
            vmem((views_n, 2, 2 * width, 2 * width), BF16),
            dma((others,)), dma((others,)),
            dma((2 * ITERS - 1,)), dma((2 * ITERS - 1,)),
            dma((views_n, others)), dma((views_n, others)),
            dma((views_n,)), dma((views_n,)),
            dma((others,)), dma((others,)),
            dma((1,)), dma((1,)),
            dma((others,)), dma((others,)),
        ],
        compiler_params=pltpu.CompilerParams(
            collective_id=0, has_side_effects=True, vmem_limit_bytes=48 * 1024 * 1024
        ),
    )(estimate.reshape(depth, blocks_n, block_rows, width), views, meta, psf_rows, psf_cols)
    return out.reshape(depth, tile_rows, width)


def solution(mesh):
    placed = (
        P(None, "gx", "gy"),
        P(None, None, "gx", "gy"),
        P(),
        P(),
        P(None, "gx"),
        P(None, "gx", "gy"),
    )
    gx_n, gy_n = mesh.shape["gx"], mesh.shape["gy"]

    def body(estimate, views, *rest):
        parts_n = 2 * estimate.shape[0]
        if gy_n == parts_n and gx_n % 2 == 0 and rest[2].shape[1] == 16:
            return band_body(gx_n, gy_n, estimate, views, *rest)
        return tile_body(estimate, views, *rest)

    return jax.shard_map(
        body, mesh=mesh, in_specs=placed, out_specs=P(None, "gx", "gy"), check_vma=False
    )
```

profile of v0, /device:TPU:0, one launch (start us, length us, event | category | flops | bytes accessed | tf_op | source)
XLA Modules:
  0.0 47.4 jit_solution(14469102082055385162)
XLA Ops:
  0.0 0.0 copy-start.4
  0.0 0.7 %convert_element_type.10 = f32[4,16]{1,0:T(4,128)S(1)} convert(s32[4,16]{1,0:T(4,128)} %param.10) | non-fusion elementwise | flops 64 | bytes 512 | tf_op jit(solution)/shard_map/convert_element_type | solution.py:404
  0.7 0.0 copy-done.4
  0.7 0.1 copy.8
  0.8 0.0 copy-start.2
  0.8 0.0 copy-start.3
  0.8 0.7 %copy-done.2 = f32[4,31]{1,0:T(4,128)S(1)} copy-done((f32[4,31]{1,0:T(4,128)S(1)}, f32[4,31]{1,0:T(4,128)}, u32[]{:S(2)}) %copy-start.2) | copy-done | bytes 520
  1.5 0.0 copy-done.3
  1.5 0.0 copy-start
  1.5 0.9 %copy-done = bf16[4,2,128,128]{3,2,1,0:T(8,128)(2,1)S(1)} copy-done((bf16[4,2,128,128]{3,2,1,0:T(8,128)(2,1)S(1)}, bf16[4,2,128,128]{3,2,1,0:T(8,128)(2,1)}, u32[]{:S(2)}) %copy-start) | copy-done | bytes 262168
  2.4 0.0 copy-start.1
  2.4 0.9 %copy-done.1 = f32[2,128,128]{2,1,0:T(8,128)S(1)} copy-done((f32[2,128,128]{2,1,0:T(8,128)S(1)}, f32[2,128,128]{2,1,0:T(8,128)}, u32[]{:S(2)}) %copy-start.1) | copy-done | bytes 131096
  3.4 43.4 %shard_map.64 = f32[2,16,8,128]{3,2,1,0:T(8,128)S(1)} custom-call(f32[2,16,8,128]{3,2,1,0:T(8,128)S(1)} %bitcast.8, bf16[4,2,128,128]{3,2,1,0:T(8,128)(2,1)S(1)} %copy-done, f32[2,8,128]{2,1,0:T(8,128)S(1)} %pad_bitcast_fusion.meta_ref, f32[4,31]{1,0:T(4,128)S(1)} %copy-done.2, f32[4,31]{1,0:T(4,128)S(1)} %copy-done.3), custom_call_target="tpu_custom_call" | custom-call | tf_op jit(solution)/shard_map/pallas_call | solution.py:413
  46.7 0.7 %copy.10 = f32[2,128,128]{2,1,0:T(8,128)} copy(f32[2,128,128]{2,1,0:T(8,128)S(1)} %bitcast.7) | data formatting | bytes 262144
  (3 shorter events, 0.0 us)
Async XLA Ops:
  0.0 0.7 %copy-start.4 = (s32[4,16,1]{1,2,0:T(1,128)S(1)}, s32[4,16,1]{1,2,0:T(1,128)}, u32[]{:S(2)}) copy-start(s32[4,16,1]{1,2,0:T(1,128)} %param.11) | copy-start | bytes 772
  0.8 0.7 %copy-start.2 = (f32[4,31]{1,0:T(4,128)S(1)}, f32[4,31]{1,0:T(4,128)}, u32[]{:S(2)}) copy-start(f32[4,31]{1,0:T(4,128)} %psf_rows_ref.1) | copy-start | bytes 1492
  0.8 0.7 %copy-start.3 = (f32[4,31]{1,0:T(4,128)S(1)}, f32[4,31]{1,0:T(4,128)}, u32[]{:S(2)}) copy-start(f32[4,31]{1,0:T(4,128)} %psf_cols_ref.1) | copy-start | bytes 1492
  1.5 0.9 %copy-start = (bf16[4,2,128,128]{3,2,1,0:T(8,128)(2,1)S(1)}, bf16[4,2,128,128]{3,2,1,0:T(8,128)(2,1)}, u32[]{:S(2)}) copy-start(bf16[4,2,128,128]{3,2,1,0:T(8,128)(2,1)} %views_ref.1) | copy-start | bytes 786436
  2.4 0.9 %copy-start.1 = (f32[2,128,128]{2,1,0:T(8,128)S(1)}, f32[2,128,128]{2,1,0:T(8,128)}, u32[]{:S(2)}) copy-start(f32[2,128,128]{2,1,0:T(8,128)} %param.6) | copy-start | bytes 393220
where the time goes:
time: 47.6 us; the launch traced here: 47.4 us
  Pallas kernels  43.4 us (91%)
  local copies, waits for them, and re-layouts  3.28 us (7%)
  other arithmetic  0.71 us (1%)
    pallas_call x1, Pallas kernels, band_body(): pl.pallas_call(functools.partial(kernel, gx_n, gy_n), out_shape=jax.Shape...  43.4 us
    unnamed x12, local copies, waits for them, and re-layouts  3.28 us

commit v1 on v0

--- a/solution.py
+++ b/solution.py
@@ -113,39 +113,39 @@
     return estimate
 
 
-def split_store(ref, index, value):
-    high = value.astype(BF16)
-    ref[(0,) + index] = high
-    ref[(1,) + index] = (value - high.astype(F32)).astype(BF16)
-
-
-def product(left, right, dims):
-    return lax.dot_general(left, right, (dims, ((), ())), preferred_element_type=F32)
-
-
 def split(value):
     high = value.astype(BF16)
     return high, (value - high.astype(F32)).astype(BF16)
 
 
+def store_terms(ref, rows, cols, axis, step, value):
+    high, low = split(value)
+    for k, part in enumerate((high, high, low)):
+        if axis == 0:
+            ref[pl.ds(rows + k * step, value.shape[0]), pl.ds(cols, value.shape[1])] = part
+        else:
+            ref[pl.ds(rows, value.shape[0]), pl.ds(cols + k * step, value.shape[1])] = part
+
+
+def terms(value, axis):
+    high, low = split(value)
+    return jnp.concatenate([high, low, high], axis=axis)
+
+
+def product(left, right):
+    return lax.dot_general(left, right, (((1,), (0,)), ((), ())), preferred_element_type=F32)
+
+
 def rows_by(band, field):
-    high, low = split(field)
-    dims = ((1,), (0,))
-    return (
-        product(band[0], high, dims) + product(band[0], low, dims) + product(band[1], high, dims)
-    )
-
-
-def cols_by(field, band, side):
-    width = band.shape[-1] // 2
+    return product(band[...], terms(field, 0))
+
+
+def cols_by(field, band):
+    width = band.shape[1] // 2
     rows = field.shape[0]
     count = field.shape[1] // width - 1
-    high, low = split(field)
-    windows = [part[:, j * width : (j + 2) * width] for part in (high, low) for j in range(count)]
-    dims = ((1,), (side,))
-    first = product(jnp.concatenate(windows, axis=0), band[0], dims)
-    second = product(jnp.concatenate(windows[:count], axis=0), band[1], dims)
-    done = first[: count * rows] + first[count * rows :] + second
+    windows = [field[:, j * width : (j + 2) * width] for j in range(count)]
+    done = product(terms(jnp.concatenate(windows, axis=0), 1), band[...])
     done = [done[j * rows : (j + 1) * rows] for j in range(count)]
     lane = lax.broadcasted_iota(jnp.int32, (rows, width), 1)
     tiles = [done[0][:, :width]]
@@ -168,10 +168,11 @@
 
 
 def kernel(
-    gx_n, gy_n, est_ref, views_ref, meta_ref, psf_rows_ref, psf_cols_ref, out_ref,
+    gx_n, gy_n, est_hbm, views_hbm, shifts_hbm, codes_hbm, psf_rows_hbm, psf_cols_hbm, out_ref,
+    est_ref, views_ref, shifts_ref, codes_ref, psf_rows_ref, psf_cols_ref, meta_wide, meta_ref,
     est_band, views_out, views_band, meta_band, lines, frac_full, shift_full, out_own, out_in,
-    band_fwd, band_back, band_cols,
-    gather_s, gather_r, halo_s, halo_r, views_s, views_r, near_s, near_r,
+    band_fwd, band_back, cols_fwd, cols_back,
+    local, gather_s, gather_r, halo_s, halo_r, views_s, views_r, near_s, near_r,
     meta_s, meta_r, edge_s, edge_r, out_s, out_r,
 ):
     views_n, depth, _, width = views_ref.shape
@@ -202,14 +203,27 @@
         pending.append(copy)
         return copy
 
+    loads = [
+        pltpu.make_async_copy(src, dst, local.at[k])
+        for k, (src, dst) in enumerate(
+            (
+                (codes_hbm, codes_ref), (shifts_hbm, shifts_ref), (est_hbm, est_ref),
+                (views_hbm, views_ref), (psf_rows_hbm, psf_rows_ref), (psf_cols_hbm, psf_cols_ref),
+            )
+        )
+    ]
+    for load in loads:
+        load.start()
     barrier = pltpu.get_barrier_semaphore()
     for target in [{"gy": p} for p in peers] + [beside]:
         pl.semaphore_signal(barrier, inc=1, device_id=target, device_id_type=MESH)
-    for view in range(views_n):
-        for layer in range(depth):
-            views_out[view, layer] = (
-                views_ref[view, layer].astype(F32).reshape(blocks_n, block_rows, width)
-            )
+    meta_wide[...] = jnp.zeros(meta_wide.shape, F32)
+    for load in loads[:2]:
+        load.wait()
+    meta_wide[pl.ds(0, views_n), pl.ds(0, blocks_n)] = codes_ref[...].astype(F32) / 16.0
+    meta_wide[pl.ds(views_n, views_n), pl.ds(0, blocks_n)] = shifts_ref[...].astype(F32)
+    meta_ref[...] = meta_wide[...].T[:blocks_n].reshape(meta_ref.shape)
+    loads[2].wait()
     pl.semaphore_wait(barrier, gy_n)
 
     meta_copies = [
@@ -228,8 +242,13 @@
                 gather_s.at[k], gather_r.at[k], {"gy": p},
             )
         )
+    loads[3].wait()
     view_copies = []
     for view in range(views_n):
+        for layer in range(depth):
+            views_out[view, layer] = (
+                views_ref[view, layer].astype(F32).reshape(blocks_n, block_rows, width)
+            )
         copies = []
         for k, p in enumerate(peers):
             layer, other = place_of(p)
@@ -248,6 +267,39 @@
             view, plane, pl.ds((part_n - NEAR) * h, view_n)
         ]
 
+    for load in loads[4:]:
+        load.wait()
+    first_row = jnp.where((g == 0) & (h == 0), 0, -HALO * block_rows)
+    last_row = jnp.where((g == gx_n - 1) & (h == 1), part_rows, part_rows + HALO * block_rows)
+    for view in range(views_n):
+        taps, total = taps_of(psf_rows_ref, view)
+        row = lax.broadcasted_iota(jnp.int32, (near_rows, band_rows), 0) - NEAR * block_rows
+        col = lax.broadcasted_iota(jnp.int32, (near_rows, band_rows), 1) - HALO * block_rows
+        inside = (col >= first_row) & (col < last_row)
+        outer = (row < first_row) | (row >= last_row)
+        value = jnp.where(inside | outer, banded(taps, total, col - row + half), 0.0)
+        store_terms(band_fwd.at[view], 0, 0, 1, band_rows, value)
+        row = lax.broadcasted_iota(jnp.int32, (part_rows, near_rows), 0)
+        col = lax.broadcasted_iota(jnp.int32, (part_rows, near_rows), 1) - NEAR * block_rows
+        inside = (col >= first_row) & (col < last_row)
+        value = jnp.where(inside, banded(taps, total, row - col + half), 0.0)
+        store_terms(band_back.at[view], 0, 0, 1, near_rows, value)
+        taps, total = taps_of(psf_cols_ref, view)
+        for ref, sign in ((cols_fwd.at[view], 1), (cols_back.at[view], -1)):
+            row = lax.broadcasted_iota(jnp.int32, (width, width), 0)
+            col = lax.broadcasted_iota(jnp.int32, (width, width), 1)
+            value = banded(taps, total, sign * (row - col) + half)
+            store_terms(ref, 0, 0, 0, 2 * width, value)
+            store_terms(ref, width, width, 0, 2 * width, value)
+            row, col = row[:16], col[:16]
+            blank = jnp.zeros((width - 16, width), F32)
+            value = banded(taps, total, sign * (row + width - col) + half)
+            value = jnp.concatenate([value, blank], axis=0)
+            store_terms(ref, width, 0, 0, 2 * width, value)
+            value = banded(taps, total, sign * (row - 16 - col) + half)
+            value = jnp.concatenate([blank, value], axis=0)
+            store_terms(ref, 0, width, 0, 2 * width, value)
+
     for copy in meta_copies:
         copy.wait_recv()
     edge = send(
@@ -260,35 +312,6 @@
         est_band.at[0, :, pl.ds((part_n + HALO) * (1 - h), HALO)],
         halo_s.at[0], halo_r.at[0], beside,
     )
-
-    first_row = jnp.where((g == 0) & (h == 0), 0, -HALO * block_rows)
-    last_row = jnp.where((g == gx_n - 1) & (h == 1), part_rows, part_rows + HALO * block_rows)
-    for view in range(views_n):
-        taps, total = taps_of(psf_rows_ref, view)
-        row = lax.broadcasted_iota(jnp.int32, (near_rows, band_rows), 0) - NEAR * block_rows
-        col = lax.broadcasted_iota(jnp.int32, (near_rows, band_rows), 1) - HALO * block_rows
-        inside = (col >= first_row) & (col < last_row)
-        outer = (row < first_row) | (row >= last_row)
-        value = banded(taps, total, col - row + half)
-        split_store(band_fwd.at[view], (), jnp.where(inside | outer, value, 0.0))
-        row = lax.broadcasted_iota(jnp.int32, (part_rows, near_rows), 0)
-        col = lax.broadcasted_iota(jnp.int32, (part_rows, near_rows), 1) - NEAR * block_rows
-        inside = (col >= first_row) & (col < last_row)
-        value = banded(taps, total, row - col + half)
-        split_store(band_back.at[view], (), jnp.where(inside, value, 0.0))
-        taps, total = taps_of(psf_cols_ref, view)
-        row = lax.broadcasted_iota(jnp.int32, (width, width), 0)
-        col = lax.broadcasted_iota(jnp.int32, (width, width), 1)
-        value = banded(taps, total, row - col + half)
-        low, high = pl.ds(0, width), pl.ds(width, width)
-        split_store(band_cols.at[view], (low, low), value)
-        split_store(band_cols.at[view], (high, high), value)
-        row, col = row[:16], col[:16]
-        blank = jnp.zeros((width - 16, width), F32)
-        value = banded(taps, total, row + width - col + half)
-        split_store(band_cols.at[view], (high, low), jnp.concatenate([value, blank], axis=0))
-        value = banded(taps, total, row - 16 - col + half)
-        split_store(band_cols.at[view], (low, high), jnp.concatenate([blank, value], axis=0))
 
     edge.wait_recv()
     for j in range(gy_n):
@@ -343,14 +366,14 @@
                 following = pltpu.roll(moved, width - 1, 1)
                 parts.append((1.0 - fraction) * moved + fraction * following)
             rows_done = rows_by(band_fwd.at[view], jnp.concatenate(parts, axis=1))
-            blurred = cols_by(rows_done, band_cols.at[view], 0)
+            blurred = cols_by(rows_done, cols_fwd.at[view])
             if sweep == 0:
                 near.wait_recv()
             ratio = [
                 views_band[view, j].reshape(near_rows, width) / blurred[j] for j in range(gy_n)
             ]
             rows_back = rows_by(band_back.at[view], jnp.concatenate(ratio, axis=1))
-            back = cols_by(rows_back, band_cols.at[view], 1)
+            back = cols_by(rows_back, cols_back.at[view])
             lane = lax.broadcasted_iota(jnp.int32, (part_rows, width), 1)
             returned = []
             for j in range(gy_n):
@@ -400,9 +423,6 @@
     views_n, depth, tile_rows, width = views.shape
     blocks_n = shifts.shape[1]
     block_rows = tile_rows // blocks_n
-    fraction = codes[:, :, 0].astype(F32) / 16.0
-    meta = jnp.concatenate([fraction, shifts.astype(F32)], axis=0).T
-    meta = jnp.pad(meta, ((0, 0), (0, width - 2 * views_n))).reshape(2, 8, width)
     part_n = blocks_n // 2
     part_rows = part_n * block_rows
     near_rows = part_rows + 2 * NEAR * block_rows
@@ -413,10 +433,17 @@
     out = pl.pallas_call(
         functools.partial(kernel, gx_n, gy_n),
         out_shape=jax.ShapeDtypeStruct((depth, blocks_n, block_rows, width), F32),
-        in_specs=[pl.BlockSpec(memory_space=pltpu.VMEM)] * 3
-        + [pl.BlockSpec(memory_space=pltpu.SMEM)] * 2,
+        in_specs=[pl.BlockSpec(memory_space=pltpu.HBM)] * 6,
         out_specs=pl.BlockSpec(memory_space=pltpu.VMEM),
         scratch_shapes=[
+            vmem((depth, blocks_n, block_rows, width), F32),
+            vmem(views.shape, BF16),
+            vmem(shifts.shape, jnp.int32),
+            vmem((views_n, blocks_n), jnp.int32),
+            pltpu.SMEM(psf_rows.shape, F32),
+            pltpu.SMEM(psf_cols.shape, F32),
+            vmem((width, width), F32),
+            vmem((2, 8, width), F32),
             vmem((ITERS, gy_n, part_n + 2 * HALO, block_rows, width), F32),
             vmem((views_n, depth, blocks_n, block_rows, width), F32),
             vmem((views_n, gy_n, part_n + 2 * NEAR, block_rows, width), F32),
@@ -426,9 +453,11 @@
             vmem((views_n, part_n + 2 * HALO, block_rows, width), F32),
             vmem((gy_n, part_n, block_rows, width), F32),
             vmem((depth, blocks_n, block_rows, width), F32),
-            vmem((views_n, 2, near_rows, band_rows), BF16),
-            vmem((views_n, 2, part_rows, near_rows), BF16),
-            vmem((views_n, 2, 2 * width, 2 * width), BF16),
+            vmem((views_n, near_rows, 3 * band_rows), BF16),
+            vmem((views_n, part_rows, 3 * near_rows), BF16),
+            vmem((views_n, 6 * width, 2 * width), BF16),
+            vmem((views_n, 6 * width, 2 * width), BF16),
+            dma((6,)),
             dma((others,)), dma((others,)),
             dma((2 * ITERS - 1,)), dma((2 * ITERS - 1,)),
             dma((views_n, others)), dma((views_n, others)),
@@ -438,9 +467,12 @@
             dma((others,)), dma((others,)),
         ],
         compiler_params=pltpu.CompilerParams(
-            collective_id=0, has_side_effects=True, vmem_limit_bytes=48 * 1024 * 1024
+            collective_id=0, has_side_effects=True, vmem_limit_bytes=60 * 1024 * 1024
         ),
-    )(estimate.reshape(depth, blocks_n, block_rows, width), views, meta, psf_rows, psf_cols)
+    )(
+        estimate.reshape(depth, blocks_n, block_rows, width), views, shifts,
+        codes.reshape(views_n, blocks_n), psf_rows, psf_cols,
+    )
     return out.reshape(depth, tile_rows, width)
 
 

time: 47.6 us -> 45.3 us (0.952)
  local copies, waits for them, and re-layouts: 3.28 us -> 1.57 us
  other arithmetic: 0.71 us -> 0 us
    unnamed x12 -> x1, local copies, waits for them, and re-layouts: 3.28 us -> 1.57 us
    convert_element_type x1 -> x0, other arithmetic: 0.7 us -> none  [band_body(): meta = jnp.concatenate([fraction, shifts.astype(F32)], axis=0).T]
where the time goes in v1:
time: 45.3 us; the launch traced here: 45.2 us
  Pallas kernels  43.6 us (96%)
  local copies, waits for them, and re-layouts  1.57 us (3%)
    pallas_call x1, Pallas kernels, band_body(): pl.pallas_call(functools.partial(kernel, gx_n, gy_n), out_shape=jax.Shape...  43.6 us
    unnamed x1, local copies, waits for them, and re-layouts  1.57 us

profile of v1, /device:TPU:0, one launch (start us, length us, event | category | flops | bytes accessed | tf_op | source)
XLA Modules:
  0.0 45.2 jit_solution(10275487538611809490)
XLA Ops:
  0.0 43.6 %shard_map.64 = f32[2,16,8,128]{3,2,1,0:T(8,128)} custom-call(f32[2,16,8,128]{3,2,1,0:T(8,128)} %bitcast.4, bf16[4,2,128,128]{3,2,1,0:T(8,128)(2,1)} %views_hbm.1, s32[4,16]{1,0:T(4,128)} %shifts_hbm.1, s32[4,16]{1,0:T(4,128)} %bitcast.5, f32[4,31]{1,0:T(4,128)} %psf_rows_hbm.1, f32[4,31]{1,0:T(4,128)} %psf_cols_hbm.1), custom_call_target="tpu_custom_call" | custom-call | tf_op jit(solution)/shard_map/pallas_call | solution.py:433
  43.6 1.6 %copy.8 = f32[2,128,128]{2,1,0:T(8,128)} copy(f32[2,128,128]{2,1,0:T(8,128)} %bitcast.3) | data formatting | bytes 262144

commit v2 on v1

--- a/solution.py
+++ b/solution.py
@@ -231,7 +231,6 @@
         for k, p in enumerate(peers)
     ]
     est_n = part_n + HALO
-    view_n = part_n + NEAR
     gathers = []
     for k, p in enumerate(peers):
         layer, other = place_of(p)
@@ -243,29 +242,32 @@
             )
         )
     loads[3].wait()
-    view_copies = []
     for view in range(views_n):
         for layer in range(depth):
             views_out[view, layer] = (
                 views_ref[view, layer].astype(F32).reshape(blocks_n, block_rows, width)
             )
+    seen = pl.ds(NEAR, part_n)
+    view_copies = []
+
+    def send_view(view):
         copies = []
         for k, p in enumerate(peers):
             layer, other = place_of(p)
             copies.append(
                 send(
-                    views_out.at[view, layer, pl.ds((part_n - NEAR) * other, view_n)],
-                    views_band.at[view, c, pl.ds(NEAR - NEAR * other, view_n)],
+                    views_out.at[view, layer, pl.ds(part_n * other, part_n)],
+                    views_band.at[view, c, seen],
                     views_s.at[view, k], views_r.at[view, k], {"gy": p},
                 )
             )
         view_copies.append(copies)
+
+    send_view(0)
     meta_band[c, pl.ds(1, 2)] = meta_ref[...]
     est_band[0, c, pl.ds(HALO - HALO * h, est_n)] = est_ref[plane, pl.ds(HALO * h, est_n)]
     for view in range(views_n):
-        views_band[view, c, pl.ds(NEAR - NEAR * h, view_n)] = views_out[
-            view, plane, pl.ds((part_n - NEAR) * h, view_n)
-        ]
+        views_band[view, c, seen] = views_out[view, plane, pl.ds(part_n * h, part_n)]
 
     for load in loads[4:]:
         load.wait()
@@ -312,6 +314,7 @@
         est_band.at[0, :, pl.ds((part_n + HALO) * (1 - h), HALO)],
         halo_s.at[0], halo_r.at[0], beside,
     )
+    send_view(1)
 
     edge.wait_recv()
     for j in range(gy_n):
@@ -350,11 +353,21 @@
             if sweep == 0:
                 for copy in view_copies[view]:
                     copy.wait_recv()
-                near = send(
-                    views_band.at[view, :, pl.ds(NEAR + (part_n - NEAR) * h, NEAR)],
-                    views_band.at[view, :, pl.ds((part_n + NEAR) * (1 - h), NEAR)],
-                    near_s.at[view], near_r.at[view], beside,
-                )
+                band = views_band.at[view]
+                nears = [
+                    send(
+                        band.at[:, pl.ds(part_n - (part_n - NEAR) * h, NEAR)],
+                        band.at[:, pl.ds((part_n + NEAR) * h, NEAR)],
+                        near_s.at[view, 0], near_r.at[view, 0], partner,
+                    ),
+                    send(
+                        band.at[:, pl.ds(NEAR + (part_n - NEAR) * h, NEAR)],
+                        band.at[:, pl.ds((part_n + NEAR) * (1 - h), NEAR)],
+                        near_s.at[view, 1], near_r.at[view, 1], beside,
+                    ),
+                ]
+                if view + 2 < views_n:
+                    send_view(view + 2)
             shift = shift_full[view]
             lane = lax.broadcasted_iota(jnp.int32, (band_rows, width), 1)
             tiles = [est_band[sweep, j] for j in range(gy_n)]
@@ -368,7 +381,8 @@
             rows_done = rows_by(band_fwd.at[view], jnp.concatenate(parts, axis=1))
             blurred = cols_by(rows_done, cols_fwd.at[view])
             if sweep == 0:
-                near.wait_recv()
+                for copy in nears:
+                    copy.wait_recv()
             ratio = [
                 views_band[view, j].reshape(near_rows, width) / blurred[j] for j in range(gy_n)
             ]
@@ -461,7 +475,7 @@
             dma((others,)), dma((others,)),
             dma((2 * ITERS - 1,)), dma((2 * ITERS - 1,)),
             dma((views_n, others)), dma((views_n, others)),
-            dma((views_n,)), dma((views_n,)),
+            dma((views_n, 2)), dma((views_n, 2)),
             dma((others,)), dma((others,)),
             dma((1,)), dma((1,)),
             dma((others,)), dma((others,)),

time: 45.3 us -> 43.6 us (0.962)
  Pallas kernels: 43.6 us -> 41.9 us
    pallas_call x1, Pallas kernels: 43.6 us -> 41.9 us  [band_body(): pl.pallas_call(functools.partial(kernel, gx_n, gy_n), out_shape=jax.Shape...]
where the time goes in v2:
time: 43.6 us; the launch traced here: 43.5 us
  Pallas kernels  41.9 us (96%)
  local copies, waits for them, and re-layouts  1.57 us (4%)
    pallas_call x1, Pallas kernels, band_body(): pl.pallas_call(functools.partial(kernel, gx_n, gy_n), out_shape=jax.Shape...  41.9 us
    unnamed x1, local copies, waits for them, and re-layouts  1.57 us

profile of v2, /device:TPU:0, one launch (start us, length us, event | category | flops | bytes accessed | tf_op | source)
XLA Modules:
  0.0 43.5 jit_solution(16512702498665469455)
XLA Ops:
  0.0 41.9 %shard_map.64 = f32[2,16,8,128]{3,2,1,0:T(8,128)} custom-call(f32[2,16,8,128]{3,2,1,0:T(8,128)} %bitcast.4, bf16[4,2,128,128]{3,2,1,0:T(8,128)(2,1)} %views_hbm.1, s32[4,16]{1,0:T(4,128)} %shifts_hbm.1, s32[4,16]{1,0:T(4,128)} %bitcast.5, f32[4,31]{1,0:T(4,128)} %psf_rows_hbm.1, f32[4,31]{1,0:T(4,128)} %psf_cols_hbm.1), custom_call_target="tpu_custom_call" | custom-call | tf_op jit(solution)/shard_map/pallas_call | solution.py:447
  41.9 1.6 %copy.8 = f32[2,128,128]{2,1,0:T(8,128)} copy(f32[2,128,128]{2,1,0:T(8,128)} %bitcast.3) | data formatting | bytes 262144

commit v3 on v2

--- a/solution.py
+++ b/solution.py
@@ -347,58 +347,111 @@
         return value
 
     own = pl.ds(HALO, part_n)
-    for sweep in range(ITERS):
-        sums = None
-        for view in range(views_n):
-            if sweep == 0:
-                for copy in view_copies[view]:
-                    copy.wait_recv()
-                band = views_band.at[view]
-                nears = [
-                    send(
-                        band.at[:, pl.ds(part_n - (part_n - NEAR) * h, NEAR)],
-                        band.at[:, pl.ds((part_n + NEAR) * h, NEAR)],
-                        near_s.at[view, 0], near_r.at[view, 0], partner,
-                    ),
-                    send(
-                        band.at[:, pl.ds(NEAR + (part_n - NEAR) * h, NEAR)],
-                        band.at[:, pl.ds((part_n + NEAR) * (1 - h), NEAR)],
-                        near_s.at[view, 1], near_r.at[view, 1], beside,
-                    ),
-                ]
-                if view + 2 < views_n:
-                    send_view(view + 2)
-            shift = shift_full[view]
-            lane = lax.broadcasted_iota(jnp.int32, (band_rows, width), 1)
-            tiles = [est_band[sweep, j] for j in range(gy_n)]
-            parts = []
-            for j in range(gy_n):
-                moved = pick(shift, tiles, j, 1).reshape(band_rows, width)
-                fraction = frac_full[view, j].reshape(band_rows, width)
-                fraction = jnp.where(lane < width - 1, fraction, 0.0)
-                following = pltpu.roll(moved, width - 1, 1)
-                parts.append((1.0 - fraction) * moved + fraction * following)
-            rows_done = rows_by(band_fwd.at[view], jnp.concatenate(parts, axis=1))
-            blurred = cols_by(rows_done, cols_fwd.at[view])
-            if sweep == 0:
-                for copy in nears:
-                    copy.wait_recv()
-            ratio = [
-                views_band[view, j].reshape(near_rows, width) / blurred[j] for j in range(gy_n)
-            ]
-            rows_back = rows_by(band_back.at[view], jnp.concatenate(ratio, axis=1))
-            back = cols_by(rows_back, cols_back.at[view])
-            lane = lax.broadcasted_iota(jnp.int32, (part_rows, width), 1)
+
+    def viewed(sweep, view, start, count):
+        place = pl.ds(start, count)
+        rows = count * block_rows
+        shift = shift_full[view, place]
+        lane = lax.broadcasted_iota(jnp.int32, (rows, width), 1)
+        tiles = [est_band[sweep, j, place] for j in range(gy_n)]
+        parts = []
+        for j in range(gy_n):
+            moved = pick(shift, tiles, j, 1).reshape(rows, width)
+            fraction = frac_full[view, j, place].reshape(rows, width)
+            fraction = jnp.where(lane < width - 1, fraction, 0.0)
+            following = pltpu.roll(moved, width - 1, 1)
+            parts.append((1.0 - fraction) * moved + fraction * following)
+        return jnp.concatenate(parts, axis=1)
+
+    def blur(sweep, views):
+        fields = [viewed(sweep, view, 0, part_n + 2 * HALO) for view in views]
+        fields = [rows_by(band_fwd.at[view], x) for view, x in zip(views, fields)]
+        return [cols_by(x, cols_fwd.at[view]) for view, x in zip(views, fields)]
+
+    def blur_cols_first(sweep, views, halos):
+        inner = [viewed(sweep, view, HALO, part_n) for view in views]
+        inner = [cols_by(x, cols_fwd.at[view]) for view, x in zip(views, inner)]
+        inner = [jnp.concatenate(tiles, axis=1) for tiles in inner]
+        for copy in halos:
+            copy.wait_recv()
+        cut = HALO * block_rows
+        outer = [
+            jnp.concatenate(
+                [viewed(sweep, view, 0, HALO), viewed(sweep, view, HALO + part_n, HALO)], axis=0
+            )
+            for view in views
+        ]
+        outer = [cols_by(x, cols_fwd.at[view]) for view, x in zip(views, outer)]
+        outer = [jnp.concatenate(tiles, axis=1) for tiles in outer]
+        fields = [jnp.concatenate([o[:cut], i, o[cut:]], axis=0) for i, o in zip(inner, outer)]
+        fields = [rows_by(band_fwd.at[view], x) for view, x in zip(views, fields)]
+        return [[x[:, j * width : (j + 1) * width] for j in range(gy_n)] for x in fields]
+
+    def correct(views, blurred):
+        ratio = [
+            [views_band[view, j].reshape(near_rows, width) / tiles[j] for j in range(gy_n)]
+            for view, tiles in zip(views, blurred)
+        ]
+        fields = [
+            rows_by(band_back.at[view], jnp.concatenate(tiles, axis=1))
+            for view, tiles in zip(views, ratio)
+        ]
+        back = [cols_by(x, cols_back.at[view]) for view, x in zip(views, fields)]
+        lane = lax.broadcasted_iota(jnp.int32, (part_rows, width), 1)
+        homes = []
+        for view, tiles in zip(views, back):
             returned = []
             for j in range(gy_n):
                 fraction = frac_full[view, j, own].reshape(part_rows, width)
                 kept = jnp.where(lane < width - 1, 1.0 - fraction, 1.0)
                 passed = jnp.where(lane > 0, fraction, 0.0)
-                value = kept * back[j] + passed * pltpu.roll(back[j], 1, 1)
+                value = kept * tiles[j] + passed * pltpu.roll(tiles[j], 1, 1)
                 returned.append(value.reshape(part_n, block_rows, width))
             shift = shift_full[view, own]
-            homes = [pick(shift, returned, j, -1) for j in range(gy_n)]
-            sums = homes if sums is None else [a + b for a, b in zip(sums, homes)]
+            homes.append([pick(shift, returned, j, -1) for j in range(gy_n)])
+        return homes
+
+    def add_up(all_homes):
+        return functools.reduce(lambda x, y: [a + b for a, b in zip(x, y)], all_homes)
+
+    def arrive(view):
+        for copy in view_copies[view]:
+            copy.wait_recv()
+        band = views_band.at[view]
+        nears = [
+            send(
+                band.at[:, pl.ds(part_n - (part_n - NEAR) * h, NEAR)],
+                band.at[:, pl.ds((part_n + NEAR) * h, NEAR)],
+                near_s.at[view, 0], near_r.at[view, 0], partner,
+            ),
+            send(
+                band.at[:, pl.ds(NEAR + (part_n - NEAR) * h, NEAR)],
+                band.at[:, pl.ds((part_n + NEAR) * (1 - h), NEAR)],
+                near_s.at[view, 1], near_r.at[view, 1], beside,
+            ),
+        ]
+        if view + 2 < views_n:
+            send_view(view + 2)
+        return nears
+
+    for sweep in range(ITERS):
+        if sweep == 0:
+            nears = []
+            blurred = []
+            for view in range(0, views_n, 2):
+                blurred += blur(sweep, list(range(view, min(view + 2, views_n))))
+                nears.append(arrive(view // 2))
+            homes = []
+            for view in range(views_n):
+                if len(nears) < min(view + 2, views_n):
+                    nears.append(arrive(len(nears)))
+                for copy in nears[view]:
+                    copy.wait_recv()
+                homes += correct([view], [blurred[view]])
+        else:
+            every = list(range(views_n))
+            homes = correct(every, blur_cols_first(sweep, every, halos))
+        sums = add_up(homes)
         updated = [est_band[sweep, j, own] * (sums[j] / views_n) for j in range(gy_n)]
         if sweep + 1 < ITERS:
             for j in range(gy_n):
@@ -416,8 +469,6 @@
                     halo_s.at[2 * sweep + 2], halo_r.at[2 * sweep + 2], beside,
                 ),
             ]
-            for copy in halos:
-                copy.wait_recv()
     for j in range(gy_n):
         out_own[j] = updated[j]
     place = pl.ds(part_n * h, part_n)
@@ -446,7 +497,7 @@
     dma = pltpu.SemaphoreType.DMA
     out = pl.pallas_call(
         functools.partial(kernel, gx_n, gy_n),
-        out_shape=jax.ShapeDtypeStruct((depth, blocks_n, block_rows, width), F32),
+        out_shape=pltpu.VMEM((depth, blocks_n, block_rows, width), F32),
         in_specs=[pl.BlockSpec(memory_space=pltpu.HBM)] * 6,
         out_specs=pl.BlockSpec(memory_space=pltpu.VMEM),
         scratch_shapes=[
@@ -481,7 +532,7 @@
             dma((others,)), dma((others,)),
         ],
         compiler_params=pltpu.CompilerParams(
-            collective_id=0, has_side_effects=True, vmem_limit_bytes=60 * 1024 * 1024
+            collective_id=0, has_side_effects=True, vmem_limit_bytes=56 * 1024 * 1024
         ),
     )(
         estimate.reshape(depth, blocks_n, block_rows, width), views, shifts,

time: 43.6 us -> 37.8 us (0.87)
  Pallas kernels: 41.9 us -> 36.9 us
  local copies, waits for them, and re-layouts: 1.57 us -> 0.66 us
    pallas_call x1, Pallas kernels: 41.9 us -> 36.9 us  [band_body(): pl.pallas_call(functools.partial(kernel, gx_n, gy_n), out_shape=pltpu.VME...]
    unnamed x1, local copies, waits for them, and re-layouts: 1.57 us -> 0.66 us
where the time goes in v3:
time: 37.8 us; the launch traced here: 37.6 us
  Pallas kernels  36.9 us (98%)
  local copies, waits for them, and re-layouts  0.66 us (2%)
    pallas_call x1, Pallas kernels, band_body(): pl.pallas_call(functools.partial(kernel, gx_n, gy_n), out_shape=pltpu.VME...  36.9 us

profile of v3, /device:TPU:0, one launch (start us, length us, event | category | flops | bytes accessed | tf_op | source)
XLA Modules:
  0.0 37.6 jit_solution(12240250548320673550)
XLA Ops:
  0.0 36.9 %shard_map.64 = f32[2,16,8,128]{3,2,1,0:T(8,128)S(1)} custom-call(f32[2,16,8,128]{3,2,1,0:T(8,128)} %bitcast.4, bf16[4,2,128,128]{3,2,1,0:T(8,128)(2,1)} %views_hbm.1, s32[4,16]{1,0:T(4,128)} %shifts_hbm.1, s32[4,16]{1,0:T(4,128)} %bitcast.5, f32[4,31]{1,0:T(4,128)} %psf_rows_hbm.1, f32[4,31]{1,0:T(4,128)} %psf_cols_hbm.1), custom_call_target="tpu_custom_call" | custom-call | tf_op jit(solution)/shard_map/pallas_call | solution.py:498
  36.9 0.7 %copy.8 = f32[2,128,128]{2,1,0:T(8,128)} copy(f32[2,128,128]{2,1,0:T(8,128)S(1)} %bitcast.3) | data formatting | bytes 262144

commit v4 on v3

--- a/solution.py
+++ b/solution.py
@@ -118,26 +118,32 @@
     return high, (value - high.astype(F32)).astype(BF16)
 
 
-def store_terms(ref, rows, cols, axis, step, value):
+def store_terms(ref, rows, cols, step, value):
     high, low = split(value)
     for k, part in enumerate((high, high, low)):
-        if axis == 0:
-            ref[pl.ds(rows + k * step, value.shape[0]), pl.ds(cols, value.shape[1])] = part
-        else:
-            ref[pl.ds(rows, value.shape[0]), pl.ds(cols + k * step, value.shape[1])] = part
-
-
-def terms(value, axis):
+        ref[pl.ds(rows + k * step, value.shape[0]), pl.ds(cols, value.shape[1])] = part
+
+
+def terms(value):
     high, low = split(value)
-    return jnp.concatenate([high, low, high], axis=axis)
+    return jnp.concatenate([high, low, high], axis=1)
 
 
 def product(left, right):
     return lax.dot_general(left, right, (((1,), (0,)), ((), ())), preferred_element_type=F32)
 
 
+def store_halves(ref, value):
+    rows, cols = value.shape
+    for k, part in enumerate(split(value)):
+        for j in range(2):
+            ref[pl.ds(k * rows, rows), pl.ds(j * cols, cols)] = part
+
+
 def rows_by(band, field):
-    return product(band[...], terms(field, 0))
+    done = product(band[...], jnp.concatenate(split(field), axis=0))
+    rows = done.shape[0] // 2
+    return done[:rows] + done[rows:]
 
 
 def cols_by(field, band):
@@ -145,7 +151,7 @@
     rows = field.shape[0]
     count = field.shape[1] // width - 1
     windows = [field[:, j * width : (j + 2) * width] for j in range(count)]
-    done = product(terms(jnp.concatenate(windows, axis=0), 1), band[...])
+    done = product(terms(jnp.concatenate(windows, axis=0)), band[...])
     done = [done[j * rows : (j + 1) * rows] for j in range(count)]
     lane = lax.broadcasted_iota(jnp.int32, (rows, width), 1)
     tiles = [done[0][:, :width]]
@@ -280,27 +286,27 @@
         inside = (col >= first_row) & (col < last_row)
         outer = (row < first_row) | (row >= last_row)
         value = jnp.where(inside | outer, banded(taps, total, col - row + half), 0.0)
-        store_terms(band_fwd.at[view], 0, 0, 1, band_rows, value)
+        store_halves(band_fwd.at[view], value)
         row = lax.broadcasted_iota(jnp.int32, (part_rows, near_rows), 0)
         col = lax.broadcasted_iota(jnp.int32, (part_rows, near_rows), 1) - NEAR * block_rows
         inside = (col >= first_row) & (col < last_row)
         value = jnp.where(inside, banded(taps, total, row - col + half), 0.0)
-        store_terms(band_back.at[view], 0, 0, 1, near_rows, value)
+        store_halves(band_back.at[view], value)
         taps, total = taps_of(psf_cols_ref, view)
         for ref, sign in ((cols_fwd.at[view], 1), (cols_back.at[view], -1)):
             row = lax.broadcasted_iota(jnp.int32, (width, width), 0)
             col = lax.broadcasted_iota(jnp.int32, (width, width), 1)
             value = banded(taps, total, sign * (row - col) + half)
-            store_terms(ref, 0, 0, 0, 2 * width, value)
-            store_terms(ref, width, width, 0, 2 * width, value)
+            store_terms(ref, 0, 0, 2 * width, value)
+            store_terms(ref, width, width, 2 * width, value)
             row, col = row[:16], col[:16]
             blank = jnp.zeros((width - 16, width), F32)
             value = banded(taps, total, sign * (row + width - col) + half)
             value = jnp.concatenate([value, blank], axis=0)
-            store_terms(ref, width, 0, 0, 2 * width, value)
+            store_terms(ref, width, 0, 2 * width, value)
             value = banded(taps, total, sign * (row - 16 - col) + half)
             value = jnp.concatenate([blank, value], axis=0)
-            store_terms(ref, 0, width, 0, 2 * width, value)
+            store_terms(ref, 0, width, 2 * width, value)
 
     for copy in meta_copies:
         copy.wait_recv()
@@ -315,6 +321,7 @@
         halo_s.at[0], halo_r.at[0], beside,
     )
     send_view(1)
+    send_view(2)
 
     edge.wait_recv()
     for j in range(gy_n):
@@ -325,13 +332,14 @@
                 near = found[:, views_n + view : views_n + view + 1]
                 lines[view, gy_n] = jnp.broadcast_to(near, found.shape)
 
+    lane = lax.broadcasted_iota(jnp.int32, (block_rows, width), 1)
+
     def spread(b, carry):
         place = pl.ds(b + 8 - HALO + part_n * h, 1)
         for view in range(views_n):
             for j in range(gy_n):
-                frac_full[view, j, b] = jnp.broadcast_to(
-                    lines[view, j, place, :], (block_rows, width)
-                )
+                line = jnp.broadcast_to(lines[view, j, place, :], (block_rows, width))
+                frac_full[view, j, b] = jnp.where(lane < width - 1, line, 0.0)
             shift_full[view, b] = jnp.broadcast_to(
                 lines[view, gy_n, place, :], (block_rows, width)
             )
@@ -352,15 +360,13 @@
         place = pl.ds(start, count)
         rows = count * block_rows
         shift = shift_full[view, place]
-        lane = lax.broadcasted_iota(jnp.int32, (rows, width), 1)
         tiles = [est_band[sweep, j, place] for j in range(gy_n)]
         parts = []
         for j in range(gy_n):
             moved = pick(shift, tiles, j, 1).reshape(rows, width)
             fraction = frac_full[view, j, place].reshape(rows, width)
-            fraction = jnp.where(lane < width - 1, fraction, 0.0)
             following = pltpu.roll(moved, width - 1, 1)
-            parts.append((1.0 - fraction) * moved + fraction * following)
+            parts.append(moved + fraction * (following - moved))
         return jnp.concatenate(parts, axis=1)
 
     def blur(sweep, views):
@@ -397,15 +403,12 @@
             for view, tiles in zip(views, ratio)
         ]
         back = [cols_by(x, cols_back.at[view]) for view, x in zip(views, fields)]
-        lane = lax.broadcasted_iota(jnp.int32, (part_rows, width), 1)
         homes = []
         for view, tiles in zip(views, back):
             returned = []
             for j in range(gy_n):
-                fraction = frac_full[view, j, own].reshape(part_rows, width)
-                kept = jnp.where(lane < width - 1, 1.0 - fraction, 1.0)
-                passed = jnp.where(lane > 0, fraction, 0.0)
-                value = kept * tiles[j] + passed * pltpu.roll(tiles[j], 1, 1)
+                passed = frac_full[view, j, own].reshape(part_rows, width) * tiles[j]
+                value = tiles[j] - passed + pltpu.roll(passed, 1, 1)
                 returned.append(value.reshape(part_n, block_rows, width))
             shift = shift_full[view, own]
             homes.append([pick(shift, returned, j, -1) for j in range(gy_n)])
@@ -430,8 +433,8 @@
                 near_s.at[view, 1], near_r.at[view, 1], beside,
             ),
         ]
-        if view + 2 < views_n:
-            send_view(view + 2)
+        if view + 3 < views_n:
+            send_view(view + 3)
         return nears
 
     for sweep in range(ITERS):
@@ -518,8 +521,8 @@
             vmem((views_n, part_n + 2 * HALO, block_rows, width), F32),
             vmem((gy_n, part_n, block_rows, width), F32),
             vmem((depth, blocks_n, block_rows, width), F32),
-            vmem((views_n, near_rows, 3 * band_rows), BF16),
-            vmem((views_n, part_rows, 3 * near_rows), BF16),
+            vmem((views_n, 2 * near_rows, 2 * band_rows), BF16),
+            vmem((views_n, 2 * part_rows, 2 * near_rows), BF16),
             vmem((views_n, 6 * width, 2 * width), BF16),
             vmem((views_n, 6 * width, 2 * width), BF16),
             dma((6,)),

time: 37.8 us -> 37.3 us (0.987)
  Pallas kernels: 36.9 us -> 36.5 us
    pallas_call x1, Pallas kernels: 36.9 us -> 36.5 us  [band_body(): pl.pallas_call(functools.partial(kernel, gx_n, gy_n), out_shape=pltpu.VME...]
where the time goes in v4:
time: 37.3 us; the launch traced here: 37.1 us
  Pallas kernels  36.5 us (98%)
  local copies, waits for them, and re-layouts  0.66 us (2%)
    pallas_call x1, Pallas kernels, band_body(): pl.pallas_call(functools.partial(kernel, gx_n, gy_n), out_shape=pltpu.VME...  36.5 us

profile of v4, /device:TPU:0, one launch (start us, length us, event | category | flops | bytes accessed | tf_op | source)
XLA Modules:
  0.0 37.1 jit_solution(4958943025395339626)
XLA Ops:
  0.0 36.5 %shard_map.64 = f32[2,16,8,128]{3,2,1,0:T(8,128)S(1)} custom-call(f32[2,16,8,128]{3,2,1,0:T(8,128)} %bitcast.4, bf16[4,2,128,128]{3,2,1,0:T(8,128)(2,1)} %views_hbm.1, s32[4,16]{1,0:T(4,128)} %shifts_hbm.1, s32[4,16]{1,0:T(4,128)} %bitcast.5, f32[4,31]{1,0:T(4,128)} %psf_rows_hbm.1, f32[4,31]{1,0:T(4,128)} %psf_cols_hbm.1), custom_call_target="tpu_custom_call" | custom-call | tf_op jit(solution)/shard_map/pallas_call | solution.py:501
  36.5 0.7 %copy.8 = f32[2,128,128]{2,1,0:T(8,128)} copy(f32[2,128,128]{2,1,0:T(8,128)S(1)} %bitcast.3) | data formatting | bytes 262144

commit v5 on v4

--- a/solution.py
+++ b/solution.py
@@ -393,24 +393,29 @@
         fields = [rows_by(band_fwd.at[view], x) for view, x in zip(views, fields)]
         return [[x[:, j * width : (j + 1) * width] for j in range(gy_n)] for x in fields]
 
-    def correct(views, blurred):
+    def rows_back(views, blurred):
         ratio = [
             [views_band[view, j].reshape(near_rows, width) / tiles[j] for j in range(gy_n)]
             for view, tiles in zip(views, blurred)
         ]
-        fields = [
+        return [
             rows_by(band_back.at[view], jnp.concatenate(tiles, axis=1))
             for view, tiles in zip(views, ratio)
         ]
+
+    def correct(views, fields, start, count):
+        rows = count * block_rows
+        place = pl.ds(HALO + start, count)
+        fields = [x[start * block_rows : start * block_rows + rows] for x in fields]
         back = [cols_by(x, cols_back.at[view]) for view, x in zip(views, fields)]
         homes = []
         for view, tiles in zip(views, back):
             returned = []
             for j in range(gy_n):
-                passed = frac_full[view, j, own].reshape(part_rows, width) * tiles[j]
+                passed = frac_full[view, j, place].reshape(rows, width) * tiles[j]
                 value = tiles[j] - passed + pltpu.roll(passed, 1, 1)
-                returned.append(value.reshape(part_n, block_rows, width))
-            shift = shift_full[view, own]
+                returned.append(value.reshape(count, block_rows, width))
+            shift = shift_full[view, place]
             homes.append([pick(shift, returned, j, -1) for j in range(gy_n)])
         return homes
 
@@ -437,28 +442,27 @@
             send_view(view + 3)
         return nears
 
+    every = list(range(views_n))
     for sweep in range(ITERS):
         if sweep == 0:
-            nears = []
-            blurred = []
-            for view in range(0, views_n, 2):
-                blurred += blur(sweep, list(range(view, min(view + 2, views_n))))
-                nears.append(arrive(view // 2))
+            blurred = blur(sweep, every)
+            nears = [arrive(0), arrive(1)]
             homes = []
-            for view in range(views_n):
+            for view in every:
                 if len(nears) < min(view + 2, views_n):
                     nears.append(arrive(len(nears)))
                 for copy in nears[view]:
                     copy.wait_recv()
-                homes += correct([view], [blurred[view]])
+                fields = rows_back([view], [blurred[view]])
+                homes += correct([view], fields, 0, part_n)
         else:
-            every = list(range(views_n))
-            homes = correct(every, blur_cols_first(sweep, every, halos))
-        sums = add_up(homes)
-        updated = [est_band[sweep, j, own] * (sums[j] / views_n) for j in range(gy_n)]
+            fields = rows_back(every, blur_cols_first(sweep, every, halos))
+            if sweep + 1 < ITERS:
+                homes = correct(every, fields, 0, part_n)
         if sweep + 1 < ITERS:
+            sums = add_up(homes)
             for j in range(gy_n):
-                est_band[sweep + 1, j, own] = updated[j]
+                est_band[sweep + 1, j, own] = est_band[sweep, j, own] * (sums[j] / views_n)
             band = est_band.at[sweep + 1]
             halos = [
                 send(
@@ -472,14 +476,23 @@
                     halo_s.at[2 * sweep + 2], halo_r.at[2 * sweep + 2], beside,
                 ),
             ]
-    for j in range(gy_n):
-        out_own[j] = updated[j]
-    place = pl.ds(part_n * h, part_n)
-    outs = [
-        send(out_own.at[p], out_in.at[plane, place], out_s.at[k], out_r.at[k], {"gy": p})
-        for k, p in enumerate(peers)
-    ]
-    out_in[plane, place] = out_own[c]
+    outs = []
+    count = part_n // 2
+    for piece in range(2):
+        start = piece * count
+        sums = add_up(correct(every, fields, start, count))
+        for j in range(gy_n):
+            joined = est_band[ITERS - 1, j, pl.ds(HALO + start, count)]
+            out_own[piece, j] = joined * (sums[j] / views_n)
+        place = pl.ds(part_n * h + start, count)
+        outs += [
+            send(
+                out_own.at[piece, p], out_in.at[plane, place],
+                out_s.at[piece, k], out_r.at[piece, k], {"gy": p},
+            )
+            for k, p in enumerate(peers)
+        ]
+        out_in[plane, place] = out_own[piece, c]
     for copy in outs:
         copy.wait_recv()
     out_ref[...] = out_in[...]
@@ -519,7 +532,7 @@
             vmem((views_n, gy_n + 1, 4 * 8, width), F32),
             vmem((views_n, gy_n, part_n + 2 * HALO, block_rows, width), F32),
             vmem((views_n, part_n + 2 * HALO, block_rows, width), F32),
-            vmem((gy_n, part_n, block_rows, width), F32),
+            vmem((2, gy_n, part_n // 2, block_rows, width), F32),
             vmem((depth, blocks_n, block_rows, width), F32),
             vmem((views_n, 2 * near_rows, 2 * band_rows), BF16),
             vmem((views_n, 2 * part_rows, 2 * near_rows), BF16),
@@ -532,7 +545,7 @@
             dma((views_n, 2)), dma((views_n, 2)),
             dma((others,)), dma((others,)),
             dma((1,)), dma((1,)),
-            dma((others,)), dma((others,)),
+            dma((2, others)), dma((2, others)),
         ],
         compiler_params=pltpu.CompilerParams(
             collective_id=0, has_side_effects=True, vmem_limit_bytes=56 * 1024 * 1024

time: 37.3 us -> 38.1 us (1.021)
  Pallas kernels: 36.5 us -> 37.2 us
    pallas_call x1, Pallas kernels: 36.5 us -> 37.2 us  [band_body(): pl.pallas_call(functools.partial(kernel, gx_n, gy_n), out_shape=pltpu.VME...]
where the time goes in v5:
time: 38.1 us; the launch traced here: 37.9 us
  Pallas kernels  37.2 us (98%)
  local copies, waits for them, and re-layouts  0.66 us (2%)
    pallas_call x1, Pallas kernels, band_body(): pl.pallas_call(functools.partial(kernel, gx_n, gy_n), out_shape=pltpu.VME...  37.2 us

profile of v5, /device:TPU:0, one launch (start us, length us, event | category | flops | bytes accessed | tf_op | source)
XLA Modules:
  0.0 37.9 jit_solution(12414571822937933981)
XLA Ops:
  0.0 37.2 %shard_map.64 = f32[2,16,8,128]{3,2,1,0:T(8,128)S(1)} custom-call(f32[2,16,8,128]{3,2,1,0:T(8,128)} %bitcast.4, bf16[4,2,128,128]{3,2,1,0:T(8,128)(2,1)} %views_hbm.1, s32[4,16]{1,0:T(4,128)} %shifts_hbm.1, s32[4,16]{1,0:T(4,128)} %bitcast.5, f32[4,31]{1,0:T(4,128)} %psf_rows_hbm.1, f32[4,31]{1,0:T(4,128)} %psf_cols_hbm.1), custom_call_target="tpu_custom_call" | custom-call | tf_op jit(solution)/shard_map/pallas_call | solution.py:514
  37.2 0.7 %copy.8 = f32[2,128,128]{2,1,0:T(8,128)} copy(f32[2,128,128]{2,1,0:T(8,128)S(1)} %bitcast.3) | data formatting | bytes 262144

commit v6 on v4

--- a/solution.py
+++ b/solution.py
@@ -320,8 +320,8 @@
         est_band.at[0, :, pl.ds((part_n + HALO) * (1 - h), HALO)],
         halo_s.at[0], halo_r.at[0], beside,
     )
-    send_view(1)
-    send_view(2)
+    for view in range(1, views_n):
+        send_view(view)
 
     edge.wait_recv()
     for j in range(gy_n):
@@ -433,8 +433,6 @@
                 near_s.at[view, 1], near_r.at[view, 1], beside,
             ),
         ]
-        if view + 3 < views_n:
-            send_view(view + 3)
         return nears
 
     for sweep in range(ITERS):

time: 37.3 us -> 38 us (1.019)
  Pallas kernels: 36.5 us -> 37.2 us
    pallas_call x1, Pallas kernels: 36.5 us -> 37.2 us  [band_body(): pl.pallas_call(functools.partial(kernel, gx_n, gy_n), out_shape=pltpu.VME...]
where the time goes in v6:
time: 38 us; the launch traced here: 37.9 us
  Pallas kernels  37.2 us (98%)
  local copies, waits for them, and re-layouts  0.66 us (2%)
    pallas_call x1, Pallas kernels, band_body(): pl.pallas_call(functools.partial(kernel, gx_n, gy_n), out_shape=pltpu.VME...  37.2 us

profile of v6, /device:TPU:0, one launch (start us, length us, event | category | flops | bytes accessed | tf_op | source)
XLA Modules:
  0.0 37.9 jit_solution(13764949582213780564)
XLA Ops:
  0.0 37.2 %shard_map.64 = f32[2,16,8,128]{3,2,1,0:T(8,128)S(1)} custom-call(f32[2,16,8,128]{3,2,1,0:T(8,128)} %bitcast.4, bf16[4,2,128,128]{3,2,1,0:T(8,128)(2,1)} %views_hbm.1, s32[4,16]{1,0:T(4,128)} %shifts_hbm.1, s32[4,16]{1,0:T(4,128)} %bitcast.5, f32[4,31]{1,0:T(4,128)} %psf_rows_hbm.1, f32[4,31]{1,0:T(4,128)} %psf_cols_hbm.1), custom_call_target="tpu_custom_call" | custom-call | tf_op jit(solution)/shard_map/pallas_call | solution.py:499
  37.2 0.7 %copy.8 = f32[2,128,128]{2,1,0:T(8,128)} copy(f32[2,128,128]{2,1,0:T(8,128)S(1)} %bitcast.3) | data formatting | bytes 262144
